TPU v7x, 768 devices: a whole 4x8x12 slice. The times are simulated.
768 devices in a mesh: row: 8 (over y), col: 24 (over z, core), inner: 4 (over x).
Axes of the slice: x: 4, y: 8, z: 12, core: 2. Of those that a mesh axis runs over, the one named last changes fastest.
Arguments:
- pattern: int32 [1536, 7], P(('row', 'col', 'inner')), may hold values from 0 to 1, as said below
- density: bfloat16 [1536, 7, 128, 128], P(('row', 'col', 'inner')), may hold values from -0.25 to 1.25, as said below
Outputs:
- purified: bfloat16 [1536, 7, 128, 128], P(('row', 'col', 'inner'))
- occupation: float32 [2], replicated
Inputs may be any that keep to these rules, and one draw needn't show every extreme that they name: pattern[i, 3] is 1; pattern[i, s] is 0 where block column i + s - 3 lies outside the matrix; pattern is symmetric: pattern[i, s] = pattern[i + s - 3, 6 - s]. density is symmetric as a matrix and its blocks are zero where pattern is 0.
All inputs are finite; a program needn't handle non-finite values.
Results may differ from a plain program's by a relative error of at most 0.02.
Values may be sent and summed in bfloat16 or wider, within the bound.
A program may use at most 32 MiB of HBM per device.

v0:
```python
import jax
import jax.numpy as jnp
from jax import lax
from jax.sharding import PartitionSpec as P

BLK = 128
REACH = 3
STEPS = 2


def from_behind(value, axis, steps):
    count = lax.axis_size(axis)
    initial, last = (max(0, -steps), min(count, count - steps))
    return lax.ppermute(value, axis, [(source, source + steps) for source in range(initial, last)])


def send_near(band, distance):
    return from_behind(band, ("row", "col", "inner"), distance)


def send_square(band, distance):
    return from_behind(band, ("row", "col", "inner"), distance)


def gather_rows(band, depth, sender):
    rows = band.shape[0]
    neighbours = -(-depth // rows)
    pieces = [sender(band, distance) for distance in range(neighbours, 0, -1)]
    pieces.append(band)
    pieces.extend([sender(band, -distance) for distance in range(1, neighbours + 1)])
    joined = jnp.concatenate(pieces, axis=0)
    offset_start = neighbours * rows - depth
    return joined[offset_start : offset_start + rows + 2 * depth]


def contract(left, right):
    return lax.dot_general(
        left, right, (((1, 3), (1, 2)), ((0,), (0,))), preferred_element_type=jnp.float32
    )


def square_rows(current, nearby, depth):
    rows = current.shape[0]
    results = []
    for target in range(4 * REACH + 1):
        first_slot = max(0, target - 2 * REACH)
        last_slot = min(2 * REACH, target)
        right = jnp.stack(
            [
                nearby[depth + slot - REACH : depth + slot - REACH + rows, target - slot]
                for slot in range(first_slot, last_slot + 1)
            ],
            axis=1,
        )
        results.append(contract(current[:, first_slot : last_slot + 1], right))
    return jnp.stack(results, axis=1).astype(jnp.bfloat16)


def cube_square_right(current, nearby_square):
    rows = current.shape[0]
    results = []
    for column in range(2 * REACH + 1):
        right = jnp.stack(
            [
                nearby_square[slot : slot + rows, column - slot + 2 * REACH]
                for slot in range(2 * REACH + 1)
            ],
            axis=1,
        )
        results.append(contract(current, right))
    return jnp.stack(results, axis=1)


def on_device(pattern, density):
    rows = density.shape[0]
    devices_all = lax.axis_size("row") * lax.axis_size("col") * lax.axis_size("inner")
    order = rows * BLK * devices_all
    kept = (pattern == 1)[:, :, None, None]
    current = density
    diagonal_terms = []
    for section in range(STEPS):
        depth = REACH
        nearby = gather_rows(current, depth, send_near)
        square = square_rows(current, nearby, depth)
        nearby_square = gather_rows(square, REACH, send_square)
        cube = cube_square_right(current, nearby_square)
        value = 3.0 * square[:, REACH : 3 * REACH + 1].astype(jnp.float32) - 2.0 * cube
        updated = jnp.where(kept, value, 0.0).astype(jnp.bfloat16)
        diagonal_terms.append(
            jnp.sum(jnp.diagonal(updated[:, REACH], axis1=1, axis2=2).astype(jnp.float32))
        )
        current = updated
    totals = lax.psum(jnp.stack(diagonal_terms), ("row", "col", "inner"))
    return (current, totals / order)


def solution(mesh):
    return jax.shard_map(
        on_device,
        mesh=mesh,
        in_specs=(P(("row", "col", "inner"), None), P(("row", "col", "inner"), None, None, None)),
        out_specs=(P(("row", "col", "inner"), None, None, None), P()),
        check_vma=False,
    )
```

profile of v0, /device:TPU:1, one launch (start us, length us, event | category | flops | bytes accessed | tf_op | source)
XLA Modules:
  0.0 350.2 jit_solution(12497718971558536084)
XLA Ops:
  1.9 5.5 %collective-permute-start = (bf16[2,7,128,128]{2,3,1,0:T(8,128)(2,1)S(1)}, bf16[2,7,128,128]{2,3,1,0:T(8,128)(2,1)S(1)}, u32[]{:S(2)}, u32[]{:S(2)}) collective-permute-start(bf16[2,7,128,128]{2,3,1,0:T(8,128)(2,1)S(1)} %copy.5), channel_id=1, source_target_pairs={{0,2},{1,3},{2,4},{3,5},{4,6},{5,7},{6,8},{7,9},{8,10},{9,11},{10,... | collective-permute-start | bytes 1376264 | tf_op jit(solution)/shard_map/ppermute | solution.py:14
  7.4 2.2 collective-permute-start.1
  9.6 4.6 %collective-permute-start.2 = (bf16[2,7,128,128]{2,3,1,0:T(8,128)(2,1)S(1)}, bf16[2,7,128,128]{2,3,1,0:T(8,128)(2,1)S(1)}, u32[]{:S(2)}, u32[]{:S(2)}) collective-permute-start(bf16[2,7,128,128]{2,3,1,0:T(8,128)(2,1)S(1)} %copy.5), channel_id=1, source_target_pairs={{1,0},{2,1},{3,2},{4,3},{5,4},{6,5},{7,6},{8,7},{9,8},{10,9},{11,1... | collective-permute-start | bytes 1376264 | tf_op jit(solution)/shard_map/ppermute | solution.py:14
  14.2 2.2 collective-permute-start.3
  16.5 4.6 %collective-permute-done.1 = bf16[2,7,128,128]{2,3,1,0:T(8,128)(2,1)S(1)} collective-permute-done((bf16[2,7,128,128]{2,3,1,0:T(8,128)(2,1)S(1)}, bf16[2,7,128,128]{2,3,1,0:T(8,128)(2,1)S(1)}, u32[]{:S(2)}, u32[]{:S(2)}) %collective-permute-start.1) | collective-permute-done | bytes 458784 | tf_op jit(solution)/shard_map/ppermute | solution.py:14
  22.7 11.1 %collective-permute-done.2 = bf16[2,7,128,128]{2,3,1,0:T(8,128)(2,1)S(1)} collective-permute-done((bf16[2,7,128,128]{2,3,1,0:T(8,128)(2,1)S(1)}, bf16[2,7,128,128]{2,3,1,0:T(8,128)(2,1)S(1)}, u32[]{:S(2)}, u32[]{:S(2)}) %collective-permute-start.2) | collective-permute-done | bytes 458784 | tf_op jit(solution)/shard_map/ppermute | solution.py:14
  37.8 9.7 %collective-permute-start.4 = (bf16[2,13,128,128]{2,3,0,1:T(8,128)(2,1)S(1)}, bf16[2,13,128,128]{2,3,0,1:T(8,128)(2,1)S(1)}, u32[]{:S(2)}, u32[]{:S(2)}) collective-permute-start(bf16[2,13,128,128]{2,3,0,1:T(8,128)(2,1)S(1)} %fusion.39), channel_id=1, source_target_pairs={{0,2},{1,3},{2,4},{3,5},{4,6},{5,7},{6,8},{7,9},{8,10},{9,11},{10,... | collective-permute-start | bytes 2555912 | tf_op jit(solution)/shard_map/ppermute | solution.py:14
  49.6 4.8 %collective-permute-start.6 = (bf16[2,13,128,128]{2,3,0,1:T(8,128)(2,1)S(1)}, bf16[2,13,128,128]{2,3,0,1:T(8,128)(2,1)S(1)}, u32[]{:S(2)}, u32[]{:S(2)}) collective-permute-start(bf16[2,13,128,128]{2,3,0,1:T(8,128)(2,1)S(1)} %fusion.39), channel_id=1, source_target_pairs={{1,0},{2,1},{3,2},{4,3},{5,4},{6,5},{7,6},{8,7},{9,8},{10,9},{11,1... | collective-permute-start | bytes 2555912 | tf_op jit(solution)/shard_map/ppermute | solution.py:14
  56.3 9.1 %collective-permute-done.4 = bf16[2,13,128,128]{2,3,0,1:T(8,128)(2,1)S(1)} collective-permute-done((bf16[2,13,128,128]{2,3,0,1:T(8,128)(2,1)S(1)}, bf16[2,13,128,128]{2,3,0,1:T(8,128)(2,1)S(1)}, u32[]{:S(2)}, u32[]{:S(2)}) %collective-permute-start.4) | collective-permute-done | bytes 852000 | tf_op jit(solution)/shard_map/ppermute | solution.py:14
  65.5 27.3 %collective-permute-done.5 = bf16[2,13,128,128]{2,3,0,1:T(8,128)(2,1)S(1)} collective-permute-done((bf16[2,13,128,128]{2,3,0,1:T(8,128)(2,1)S(1)}, bf16[2,13,128,128]{2,3,0,1:T(8,128)(2,1)S(1)}, u32[]{:S(2)}, u32[]{:S(2)}) %collective-permute-start.5) | collective-permute-done | bytes 852000 | tf_op jit(solution)/shard_map/ppermute | solution.py:14
  93.4 6.8 %collective-permute-done.6 = bf16[2,13,128,128]{2,3,0,1:T(8,128)(2,1)S(1)} collective-permute-done((bf16[2,13,128,128]{2,3,0,1:T(8,128)(2,1)S(1)}, bf16[2,13,128,128]{2,3,0,1:T(8,128)(2,1)S(1)}, u32[]{:S(2)}, u32[]{:S(2)}) %collective-permute-start.6) | collective-permute-done | bytes 852000 | tf_op jit(solution)/shard_map/ppermute | solution.py:14
  100.5 2.4 collective-permute-done.7
  107.3 8.7 %collective-permute-start.9 = (bf16[2,7,128,128]{2,3,0,1:T(8,128)(2,1)S(1)}, bf16[2,7,128,128]{2,3,0,1:T(8,128)(2,1)S(1)}, u32[]{:S(2)}, u32[]{:S(2)}) collective-permute-start(bf16[2,7,128,128]{2,3,0,1:T(8,128)(2,1)S(1)} %select_convert_fusion.1), channel_id=1, source_target_pairs={{0,1},{1,2},{2,3},{3,4},{4,5},{5,6},{6,7},{7,8},{8,9},{9,10},{10,1... | collective-permute-start | bytes 1376264 | tf_op jit(solution)/shard_map/ppermute | solution.py:14
  116.0 5.3 %collective-permute-start.10 = (bf16[2,7,128,128]{2,3,0,1:T(8,128)(2,1)S(1)}, bf16[2,7,128,128]{2,3,0,1:T(8,128)(2,1)S(1)}, u32[]{:S(2)}, u32[]{:S(2)}) collective-permute-start(bf16[2,7,128,128]{2,3,0,1:T(8,128)(2,1)S(1)} %select_convert_fusion.1), channel_id=1, source_target_pairs={{1,0},{2,1},{3,2},{4,3},{5,4},{6,5},{7,6},{8,7},{9,8},{10,9},{11,1... | collective-permute-start | bytes 1376264 | tf_op jit(solution)/shard_map/ppermute | solution.py:14
  121.3 4.8 %collective-permute-start.11 = (bf16[2,7,128,128]{2,3,0,1:T(8,128)(2,1)S(1)}, bf16[2,7,128,128]{2,3,0,1:T(8,128)(2,1)S(1)}, u32[]{:S(2)}, u32[]{:S(2)}) collective-permute-start(bf16[2,7,128,128]{2,3,0,1:T(8,128)(2,1)S(1)} %select_convert_fusion.1), channel_id=1, source_target_pairs={{2,0},{3,1},{4,2},{5,3},{6,4},{7,5},{8,6},{9,7},{10,8},{11,9},{12,... | collective-permute-start | bytes 1376264 | tf_op jit(solution)/shard_map/ppermute | solution.py:14
  127.1 13.4 %collective-permute-done.10 = bf16[2,7,128,128]{2,3,0,1:T(8,128)(2,1)S(1)} collective-permute-done((bf16[2,7,128,128]{2,3,0,1:T(8,128)(2,1)S(1)}, bf16[2,7,128,128]{2,3,0,1:T(8,128)(2,1)S(1)}, u32[]{:S(2)}, u32[]{:S(2)}) %collective-permute-start.10) | collective-permute-done | bytes 458784 | tf_op jit(solution)/shard_map/ppermute | solution.py:14
  145.1 7.7 %collective-permute-start.13 = (bf16[2,13,128,128]{2,3,0,1:T(8,128)(2,1)S(1)}, bf16[2,13,128,128]{2,3,0,1:T(8,128)(2,1)S(1)}, u32[]{:S(2)}, u32[]{:S(2)}) collective-permute-start(bf16[2,13,128,128]{2,3,0,1:T(8,128)(2,1)S(1)} %fusion.43), channel_id=1, source_target_pairs={{0,1},{1,2},{2,3},{3,4},{4,5},{5,6},{6,7},{7,8},{8,9},{9,10},{10,1... | collective-permute-start | bytes 2555912 | tf_op jit(solution)/shard_map/ppermute | solution.py:14
  152.9 5.3 %collective-permute-start.14 = (bf16[2,13,128,128]{2,3,0,1:T(8,128)(2,1)S(1)}, bf16[2,13,128,128]{2,3,0,1:T(8,128)(2,1)S(1)}, u32[]{:S(2)}, u32[]{:S(2)}) collective-permute-start(bf16[2,13,128,128]{2,3,0,1:T(8,128)(2,1)S(1)} %fusion.43), channel_id=1, source_target_pairs={{1,0},{2,1},{3,2},{4,3},{5,4},{6,5},{7,6},{8,7},{9,8},{10,9},{11,1... | collective-permute-start | bytes 2555912 | tf_op jit(solution)/shard_map/ppermute | solution.py:14
  158.2 5.9 %collective-permute-start.15 = (bf16[2,13,128,128]{2,3,0,1:T(8,128)(2,1)S(1)}, bf16[2,13,128,128]{2,3,0,1:T(8,128)(2,1)}, u32[]{:S(2)}, u32[]{:S(2)}) collective-permute-start(bf16[2,13,128,128]{2,3,0,1:T(8,128)(2,1)S(1)} %fusion.43), channel_id=1, source_target_pairs={{2,0},{3,1},{4,2},{5,3},{6,4},{7,5},{8,6},{9,7},{10,8},{11,9},{12,... | collective-permute-start | bytes 2555912 | tf_op jit(solution)/shard_map/ppermute | solution.py:14
  164.2 7.4 %copy.87 = bf16[2,128,128]{0,2,1:T(8,128)(2,1)} copy(bf16[2,128,128]{1,2,0:T(8,128)(2,1)S(1)} %get-tuple-element.128) | data formatting | bytes 131072 | tf_op jit(solution)/shard_map/squeeze | solution.py:90
  171.6 2.0 gather_fusion
  175.9 26.5 %collective-permute-done.14 = bf16[2,13,128,128]{2,3,0,1:T(8,128)(2,1)S(1)} collective-permute-done((bf16[2,13,128,128]{2,3,0,1:T(8,128)(2,1)S(1)}, bf16[2,13,128,128]{2,3,0,1:T(8,128)(2,1)S(1)}, u32[]{:S(2)}, u32[]{:S(2)}) %collective-permute-start.14) | collective-permute-done | bytes 852000 | tf_op jit(solution)/shard_map/ppermute | solution.py:14
  206.2 7.4 %copy.88 = bf16[2,128,128]{0,2,1:T(8,128)(2,1)} copy(bf16[2,128,128]{1,2,0:T(8,128)(2,1)S(1)} %slice_bitcast_fusion) | data formatting | bytes 131072 | tf_op jit(solution)/shard_map/squeeze | solution.py:90
  218.5 131.2 %psum.7 = f32[2]{0:T(128)S(1)} all-reduce(f32[2]{0:T(128)S(1)} %pad_maximum_fusion.8), channel_id=1, replica_groups=mesh['row'=8,'col'=24,'inner'=4] {'row','col','inner'}, use_global_device_ids=true, to_apply=%region_2.3 | all-reduce | flops 2 | bytes 16 | tf_op jit(solution)/shard_map/psum | solution.py:93
  (129 shorter events, 32.8 us)
Async XLA Ops:
  1.9 14.5 %collective-permute-start = (bf16[2,7,128,128]{2,3,1,0:T(8,128)(2,1)S(1)}, bf16[2,7,128,128]{2,3,1,0:T(8,128)(2,1)S(1)}, u32[]{:S(2)}, u32[]{:S(2)}) collective-permute-start(bf16[2,7,128,128]{2,3,1,0:T(8,128)(2,1)S(1)} %copy.5), channel_id=1, source_target_pairs={{0,2},{1,3},{2,4},{3,5},{4,6},{5,7},{6,8},{7,9},{8,10},{9,11},{10,... | collective-permute-start | bytes 1376264 | tf_op jit(solution)/shard_map/ppermute | solution.py:14
  7.4 13.7 %collective-permute-start.1 = (bf16[2,7,128,128]{2,3,1,0:T(8,128)(2,1)S(1)}, bf16[2,7,128,128]{2,3,1,0:T(8,128)(2,1)S(1)}, u32[]{:S(2)}, u32[]{:S(2)}) collective-permute-start(bf16[2,7,128,128]{2,3,1,0:T(8,128)(2,1)S(1)} %copy.5), channel_id=1, source_target_pairs={{0,1},{1,2},{2,3},{3,4},{4,5},{5,6},{6,7},{7,8},{8,9},{9,10},{10,1... | collective-permute-start | bytes 1376264 | tf_op jit(solution)/shard_map/ppermute | solution.py:14
  9.6 24.1 %collective-permute-start.2 = (bf16[2,7,128,128]{2,3,1,0:T(8,128)(2,1)S(1)}, bf16[2,7,128,128]{2,3,1,0:T(8,128)(2,1)S(1)}, u32[]{:S(2)}, u32[]{:S(2)}) collective-permute-start(bf16[2,7,128,128]{2,3,1,0:T(8,128)(2,1)S(1)} %copy.5), channel_id=1, source_target_pairs={{1,0},{2,1},{3,2},{4,3},{5,4},{6,5},{7,6},{8,7},{9,8},{10,9},{11,1... | collective-permute-start | bytes 1376264 | tf_op jit(solution)/shard_map/ppermute | solution.py:14
  14.2 21.7 %collective-permute-start.3 = (bf16[2,7,128,128]{2,3,1,0:T(8,128)(2,1)S(1)}, bf16[2,7,128,128]{2,3,1,0:T(8,128)(2,1)S(1)}, u32[]{:S(2)}, u32[]{:S(2)}) collective-permute-start(bf16[2,7,128,128]{2,3,1,0:T(8,128)(2,1)S(1)} %copy.5), channel_id=1, source_target_pairs={{2,0},{3,1},{4,2},{5,3},{6,4},{7,5},{8,6},{9,7},{10,8},{11,9},{12,... | collective-permute-start | bytes 1376264 | tf_op jit(solution)/shard_map/ppermute | solution.py:14
  21.1 1.0 copy-start
  36.9 12.6 %copy-start.1 = (s32[2,7]{1,0:T(2,128)S(1)}, s32[2,7]{1,0:T(2,128)}, u32[]{:S(2)}) copy-start(s32[2,7]{1,0:T(2,128)} %param.2) | copy-start | bytes 172
  37.8 27.7 %collective-permute-start.4 = (bf16[2,13,128,128]{2,3,0,1:T(8,128)(2,1)S(1)}, bf16[2,13,128,128]{2,3,0,1:T(8,128)(2,1)S(1)}, u32[]{:S(2)}, u32[]{:S(2)}) collective-permute-start(bf16[2,13,128,128]{2,3,0,1:T(8,128)(2,1)S(1)} %fusion.39), channel_id=1, source_target_pairs={{0,2},{1,3},{2,4},{3,5},{4,6},{5,7},{6,8},{7,9},{8,10},{9,11},{10,... | collective-permute-start | bytes 2555912 | tf_op jit(solution)/shard_map/ppermute | solution.py:14
  47.5 45.3 %collective-permute-start.5 = (bf16[2,13,128,128]{2,3,0,1:T(8,128)(2,1)S(1)}, bf16[2,13,128,128]{2,3,0,1:T(8,128)(2,1)S(1)}, u32[]{:S(2)}, u32[]{:S(2)}) collective-permute-start(bf16[2,13,128,128]{2,3,0,1:T(8,128)(2,1)S(1)} %fusion.39), channel_id=1, source_target_pairs={{0,1},{1,2},{2,3},{3,4},{4,5},{5,6},{6,7},{7,8},{8,9},{9,10},{10,1... | collective-permute-start | bytes 2555912 | tf_op jit(solution)/shard_map/ppermute | solution.py:14
  49.6 50.6 %collective-permute-start.6 = (bf16[2,13,128,128]{2,3,0,1:T(8,128)(2,1)S(1)}, bf16[2,13,128,128]{2,3,0,1:T(8,128)(2,1)S(1)}, u32[]{:S(2)}, u32[]{:S(2)}) collective-permute-start(bf16[2,13,128,128]{2,3,0,1:T(8,128)(2,1)S(1)} %fusion.39), channel_id=1, source_target_pairs={{1,0},{2,1},{3,2},{4,3},{5,4},{6,5},{7,6},{8,7},{9,8},{10,9},{11,1... | collective-permute-start | bytes 2555912 | tf_op jit(solution)/shard_map/ppermute | solution.py:14
  54.4 48.4 %collective-permute-start.7 = (bf16[2,13,128,128]{2,3,0,1:T(8,128)(2,1)S(1)}, bf16[2,13,128,128]{2,3,0,1:T(8,128)(2,1)S(1)}, u32[]{:S(2)}, u32[]{:S(2)}) collective-permute-start(bf16[2,13,128,128]{2,3,0,1:T(8,128)(2,1)S(1)} %fusion.39), channel_id=1, source_target_pairs={{2,0},{3,1},{4,2},{5,3},{6,4},{7,5},{8,6},{9,7},{10,8},{11,9},{12,... | collective-permute-start | bytes 2555912 | tf_op jit(solution)/shard_map/ppermute | solution.py:14
  105.4 20.8 %collective-permute-start.8 = (bf16[2,7,128,128]{2,3,0,1:T(8,128)(2,1)S(1)}, bf16[2,7,128,128]{2,3,0,1:T(8,128)(2,1)S(1)}, u32[]{:S(2)}, u32[]{:S(2)}) collective-permute-start(bf16[2,7,128,128]{2,3,0,1:T(8,128)(2,1)S(1)} %select_convert_fusion.1), channel_id=1, source_target_pairs={{0,2},{1,3},{2,4},{3,5},{4,6},{5,7},{6,8},{7,9},{8,10},{9,11},{10,... | collective-permute-start | bytes 1376264 | tf_op jit(solution)/shard_map/ppermute | solution.py:14
  107.3 18.9 %collective-permute-start.9 = (bf16[2,7,128,128]{2,3,0,1:T(8,128)(2,1)S(1)}, bf16[2,7,128,128]{2,3,0,1:T(8,128)(2,1)S(1)}, u32[]{:S(2)}, u32[]{:S(2)}) collective-permute-start(bf16[2,7,128,128]{2,3,0,1:T(8,128)(2,1)S(1)} %select_convert_fusion.1), channel_id=1, source_target_pairs={{0,1},{1,2},{2,3},{3,4},{4,5},{5,6},{6,7},{7,8},{8,9},{9,10},{10,1... | collective-permute-start | bytes 1376264 | tf_op jit(solution)/shard_map/ppermute | solution.py:14
  116.0 24.5 %collective-permute-start.10 = (bf16[2,7,128,128]{2,3,0,1:T(8,128)(2,1)S(1)}, bf16[2,7,128,128]{2,3,0,1:T(8,128)(2,1)S(1)}, u32[]{:S(2)}, u32[]{:S(2)}) collective-permute-start(bf16[2,7,128,128]{2,3,0,1:T(8,128)(2,1)S(1)} %select_convert_fusion.1), channel_id=1, source_target_pairs={{1,0},{2,1},{3,2},{4,3},{5,4},{6,5},{7,6},{8,7},{9,8},{10,9},{11,1... | collective-permute-start | bytes 1376264 | tf_op jit(solution)/shard_map/ppermute | solution.py:14
  121.3 20.1 %collective-permute-start.11 = (bf16[2,7,128,128]{2,3,0,1:T(8,128)(2,1)S(1)}, bf16[2,7,128,128]{2,3,0,1:T(8,128)(2,1)S(1)}, u32[]{:S(2)}, u32[]{:S(2)}) collective-permute-start(bf16[2,7,128,128]{2,3,0,1:T(8,128)(2,1)S(1)} %select_convert_fusion.1), channel_id=1, source_target_pairs={{2,0},{3,1},{4,2},{5,3},{6,4},{7,5},{8,6},{9,7},{10,8},{11,9},{12,... | collective-permute-start | bytes 1376264 | tf_op jit(solution)/shard_map/ppermute | solution.py:14
  143.2 30.9 %collective-permute-start.12 = (bf16[2,13,128,128]{2,3,0,1:T(8,128)(2,1)S(1)}, bf16[2,13,128,128]{2,3,0,1:T(8,128)(2,1)}, u32[]{:S(2)}, u32[]{:S(2)}) collective-permute-start(bf16[2,13,128,128]{2,3,0,1:T(8,128)(2,1)S(1)} %fusion.43), channel_id=1, source_target_pairs={{0,2},{1,3},{2,4},{3,5},{4,6},{5,7},{6,8},{7,9},{8,10},{9,11},{10,... | collective-permute-start | bytes 2555912 | tf_op jit(solution)/shard_map/ppermute | solution.py:14
  145.1 30.2 %collective-permute-start.13 = (bf16[2,13,128,128]{2,3,0,1:T(8,128)(2,1)S(1)}, bf16[2,13,128,128]{2,3,0,1:T(8,128)(2,1)S(1)}, u32[]{:S(2)}, u32[]{:S(2)}) collective-permute-start(bf16[2,13,128,128]{2,3,0,1:T(8,128)(2,1)S(1)} %fusion.43), channel_id=1, source_target_pairs={{0,1},{1,2},{2,3},{3,4},{4,5},{5,6},{6,7},{7,8},{8,9},{9,10},{10,1... | collective-permute-start | bytes 2555912 | tf_op jit(solution)/shard_map/ppermute | solution.py:14
  152.9 49.5 %collective-permute-start.14 = (bf16[2,13,128,128]{2,3,0,1:T(8,128)(2,1)S(1)}, bf16[2,13,128,128]{2,3,0,1:T(8,128)(2,1)S(1)}, u32[]{:S(2)}, u32[]{:S(2)}) collective-permute-start(bf16[2,13,128,128]{2,3,0,1:T(8,128)(2,1)S(1)} %fusion.43), channel_id=1, source_target_pairs={{1,0},{2,1},{3,2},{4,3},{5,4},{6,5},{7,6},{8,7},{9,8},{10,9},{11,1... | collective-permute-start | bytes 2555912 | tf_op jit(solution)/shard_map/ppermute | solution.py:14
  158.2 44.4 %collective-permute-start.15 = (bf16[2,13,128,128]{2,3,0,1:T(8,128)(2,1)S(1)}, bf16[2,13,128,128]{2,3,0,1:T(8,128)(2,1)}, u32[]{:S(2)}, u32[]{:S(2)}) collective-permute-start(bf16[2,13,128,128]{2,3,0,1:T(8,128)(2,1)S(1)} %fusion.43), channel_id=1, source_target_pairs={{2,0},{3,1},{4,2},{5,3},{6,4},{7,5},{8,6},{9,7},{10,8},{11,9},{12,... | collective-permute-start | bytes 2555912 | tf_op jit(solution)/shard_map/ppermute | solution.py:14
where the time goes:
time: 351 us; the launch traced here: 350 us
  blocking collectives  131 us (37%)
  waiting for transfers between devices  102 us (29%)
  starting transfers between devices  74.6 us (21%)
  local copies, waits for them, and re-layouts  26.2 us (7%)
  matrix products  10.1 us (3%)
  other arithmetic  4.38 us (1%)
    psum x1, blocking collectives, on_device(): totals = lax.psum(jnp.stack(diagonal_terms), ('row', 'col', 'inner'))  131 us
    ppermute x16, waiting for transfers between devices, from_behind(): lax.ppermute(value, axis, [(source, source + steps) for source in range(i...  102 us
    ppermute x16, starting transfers between devices, from_behind(): lax.ppermute(value, axis, [(source, source + steps) for source in range(i...  74.6 us
    squeeze x3, local copies, waits for them, and re-layouts, on_device(): updated[:, REACH]  14.8 us
    dot_general x40, matrix products, contract(): lax.dot_general(left, right, (((1, 3), (1, 2)), ((0,), (0,))), preferred_...  10.1 us
  transfers between devices with their start and end apart: 16, of which 9 were waited for; matrix products, arithmetic and copies ran while one was open for 5% of the time, Pallas kernels for 0%

commit v1 on v0

v1 whole, which is shorter than its diff:
```python
import functools

import jax
import jax.numpy as jnp
from jax import lax
from jax.experimental import pallas as pl
from jax.experimental.pallas import tpu as pltpu
from jax.sharding import PartitionSpec as P

BLK = 128
REACH = 3
SLOTS = 7
STEPS = 2
CORES = 2
MESH = pl.DeviceIdType.MESH

WINDOW = 8
COLUMNS = WINDOW + SLOTS - 1

MESSAGES = (
    (4, 0, 4, 2, 1, None),
    (3, 3, 4, 5, -1, None),
    (3, 0, 4, 1, 1, None),
    (4, 3, 4, 6, -1, None),
    (4, 6, 1, 2, 1, None),
    (2, 0, 4, 0, 1, 0),
    (5, 3, 4, 7, -1, 1),
)
FROM_OWN = ((0, 6), (1, 5), (1, 6), (2, 4), (2, 5), (5, 1), (5, 2), (6, 0), (6, 1), (7, 0))
FROM_MESSAGE = {0: ((0, 5), (1, 4)), 1: ((6, 2), (7, 1)), 2: ((0, 4),), 3: ((7, 2),), 4: ((5, 0),)}


def kernel(
    sizes, pattern, density, purified, occupation, near0, near1, left, total, square, last,
    diagonals, sums_a, sums_b, sums_c, send_sem, recv_sem, load_sem, store_sem,
    sum_send, recv_a, recv_b, recv_c,
):
    rows, columns, inners = sizes
    count = rows * columns * inners
    row, col, inner = lax.axis_index("row"), lax.axis_index("col"), lax.axis_index("inner")
    place = (row * columns + col) * inners + inner

    def along(steps):
        other = lax.rem(place + steps + count, count)
        upper = other // inners
        return (upper // columns, lax.rem(upper, columns), lax.rem(other, inners))

    layers = columns // CORES
    layer, core = col // CORES, lax.rem(col, CORES)
    chip = core * inners + inner

    def partner_a(step):
        other = lax.rem(chip + step, CORES * inners)
        return (row, layer * CORES + other // inners, lax.rem(other, inners))

    def partner_b(step):
        return (row, lax.rem(layer + step, layers) * CORES + core, inner)

    def partner_c(step):
        return (lax.rem(row + step, rows), col, inner)

    phases = (
        (CORES * inners, chip, partner_a, sums_a, recv_a, 0),
        (layers, layer, partner_b, sums_b, recv_b, CORES * inners),
        (rows, row, partner_c, sums_c, recv_c, CORES * inners + layers),
    )

    load = pltpu.make_async_copy(density, near0.at[pl.ds(3, 2)], load_sem)
    load.start()

    barrier = pltpu.get_barrier_semaphore()
    greeted = 0
    for steps in (1, -1):
        pl.semaphore_signal(barrier, inc=1, device_id=along(steps), device_id_type=MESH)
        greeted += 1
    for size, _, partner, _, _, _ in phases:
        for step in range(1, size):
            pl.semaphore_signal(barrier, inc=1, device_id=partner(step), device_id_type=MESH)
            greeted += 1
    zero_block = jnp.zeros((BLK, BLK), jnp.bfloat16)
    left[0:BLK, 7 * BLK : 8 * BLK] = zero_block
    left[BLK : 2 * BLK, 0:BLK] = zero_block
    load.wait()
    pl.semaphore_wait(barrier, greeted)

    eye = lax.broadcasted_iota(jnp.int32, (BLK, BLK), 0) == lax.broadcasted_iota(jnp.int32, (BLK, BLK), 1)

    def block(near, r, column):
        slot = column - r
        return near[r, slot] if 0 <= slot < SLOTS else zero_block

    def tile(near, r, column, width):
        return jnp.concatenate(
            [
                jnp.concatenate([block(near, r + i, column + j) for j in range(width)], axis=1)
                for i in range(2)
            ],
            axis=0,
        )

    def mirror(near, places):
        for r, slot in places:
            near[r, slot] = near[r + slot - REACH, 2 * REACH - slot].T

    def span(column, width=2):
        return slice(column * BLK, (column + width) * BLK)

    def update(near, q, store):
        right = tile(near, 2 * q, 2 * q, 8)
        cube = lax.dot_general(
            square[:, span(2 * q, 8)], right, (((1,), (1,)), ((), ())), preferred_element_type=jnp.float32
        )
        for r in range(2):
            for j in range(2):
                slot = 2 * q + j - r
                if 0 <= slot < SLOTS:
                    mine = slice(r * BLK, (r + 1) * BLK)
                    value = (
                        3.0 * square[mine, span(2 * q + j + REACH, 1)].astype(jnp.float32)
                        - 2.0 * cube[mine, span(j, 1)]
                    )
                    store(r, slot, jnp.where(pattern[r, slot] == 1, value, 0.0).astype(jnp.bfloat16))

    def exchange(section, near):
        copies = []
        for index, (r, slot, slots, target, direction, after) in enumerate(MESSAGES):
            copies.append(
                pltpu.make_async_remote_copy(
                    src_ref=near.at[r, pl.ds(slot, slots)],
                    dst_ref=near.at[target, pl.ds(slot, slots)],
                    send_sem=send_sem.at[section, index],
                    recv_sem=recv_sem.at[section, index],
                    device_id=along(direction),
                    device_id_type=MESH,
                )
            )
            if after is None:
                copies[-1].start()
        return copies

    def squares(near, copies):
        for r in range(2):
            for slot in range(SLOTS):
                left[r * BLK : (r + 1) * BLK, span(slot + r, 1)] = near[3 + r, slot]
        mirror(near, FROM_OWN)
        copies[0].wait_recv()
        copies[5].start()
        copies[1].wait_recv()
        copies[6].start()
        mirror(near, FROM_MESSAGE[0])
        mirror(near, FROM_MESSAGE[1])
        copies[4].wait_recv()
        mirror(near, FROM_MESSAGE[4])
        for column in range(2, 12, 2):
            terms = [
                jnp.dot(left[:, span(r)], tile(near, r, column, 2), preferred_element_type=jnp.float32)
                for r in (2, 4)
                if r - 1 <= column <= r + 7
            ]
            total[:, span(column)] = functools.reduce(jnp.add, terms)
        copies[2].wait_recv()
        copies[3].wait_recv()
        mirror(near, FROM_MESSAGE[2])
        mirror(near, FROM_MESSAGE[3])
        copies[5].wait_recv()
        copies[6].wait_recv()
        for column in range(0, COLUMNS, 2):
            terms = [total[:, span(column)]] if 2 <= column < 12 else []
            terms += [
                jnp.dot(left[:, span(r)], tile(near, r, column, 2), preferred_element_type=jnp.float32)
                for r in (0, 6)
                if r - 1 <= column <= r + 7
            ]
            square[:, span(column)] = functools.reduce(jnp.add, terms).astype(jnp.bfloat16)

    copies0 = exchange(0, near0)
    squares(near0, copies0)

    def keep(r, slot, value):
        near1[3 + r, slot] = value

    for q in range(4):
        update(near0, q, keep)
    copies1 = exchange(1, near1)

    on_diagonal = sum(
        jnp.where(eye, near1[3 + r, REACH].astype(jnp.float32), 0.0) for r in range(2)
    )
    diagonals[0:1, :] = jnp.sum(on_diagonal, axis=0, keepdims=True)

    squares(near1, copies1)
    total_diagonal = jnp.zeros((1, BLK), jnp.float32)
    for r in range(2):
        mine = slice(r * BLK, (r + 1) * BLK)
        cubes = sum(
            square[mine, span(r + REACH + slot, 1)].astype(jnp.float32) * near1[3 + r, slot].astype(jnp.float32)
            for slot in range(SLOTS)
        )
        kept = jnp.where(eye, square[mine, span(2 * REACH + r, 1)].astype(jnp.float32), 0.0)
        value = 3.0 * jnp.sum(kept, axis=1, keepdims=True) - 2.0 * jnp.sum(cubes, axis=1, keepdims=True)
        value = jnp.where(pattern[r, REACH] == 1, value, 0.0).astype(jnp.bfloat16).astype(jnp.float32)
        total_diagonal += jnp.sum(jnp.where(eye, value, 0.0), axis=0, keepdims=True)
    diagonals[1:2, :] = total_diagonal

    def sum_copies(phase):
        size, me, partner, sums, arrived, first = phase
        sums[me] = diagonals[...]
        started = []
        for step in range(1, size):
            copy = pltpu.make_async_remote_copy(
                src_ref=diagonals,
                dst_ref=sums.at[me],
                send_sem=sum_send.at[first + step],
                recv_sem=arrived.at[me],
                device_id=partner(step),
                device_id_type=MESH,
            )
            copy.start()
            started.append(copy)
        return started

    def sum_wait(phase, started):
        size, me, _, sums, arrived, first = phase
        for step in range(1, size):
            other = lax.rem(me + step, size)
            pltpu.make_async_remote_copy(
                src_ref=diagonals,
                dst_ref=sums.at[other],
                send_sem=sum_send.at[first + step],
                recv_sem=arrived.at[other],
                device_id=phase[2](step),
                device_id_type=MESH,
            ).wait_recv()
        for copy in started:
            copy.wait_send()
        return functools.reduce(jnp.add, [sums[i] for i in range(size)])

    def finish(r, slot, value):
        last[r, slot] = value

    started = sum_copies(phases[0])
    update(near1, 0, finish)
    update(near1, 1, finish)
    diagonals[...] = sum_wait(phases[0], started)
    started = sum_copies(phases[1])
    update(near1, 2, finish)
    update(near1, 3, finish)
    store = pltpu.make_async_copy(last, purified, store_sem)
    store.start()
    diagonals[...] = sum_wait(phases[1], started)
    started = sum_copies(phases[2])
    for copy in copies0 + copies1:
        copy.wait_send()
    sums = sum_wait(phases[2], started)
    order = 2.0 * BLK * count
    for section in range(STEPS):
        occupation[section] = jnp.sum(sums[section : section + 1, :]) / order
    store.wait()


def on_device(sizes, pattern, density):
    rows, columns, inners = sizes
    chips, layers = CORES * inners, columns // CORES
    flat = pltpu.VMEM((WINDOW, SLOTS, BLK, BLK), jnp.bfloat16)
    wide = COLUMNS * BLK
    purified, occupation = pl.pallas_call(
        functools.partial(kernel, sizes),
        out_shape=(
            jax.ShapeDtypeStruct(density.shape, jnp.bfloat16),
            jax.ShapeDtypeStruct((STEPS,), jnp.float32),
        ),
        in_specs=[pl.BlockSpec(memory_space=pltpu.SMEM), pl.BlockSpec(memory_space=pl.ANY)],
        out_specs=(pl.BlockSpec(memory_space=pl.ANY), pl.BlockSpec(memory_space=pltpu.SMEM)),
        scratch_shapes=[
            flat,
            flat,
            pltpu.VMEM((2 * BLK, WINDOW * BLK), jnp.bfloat16),
            pltpu.VMEM((2 * BLK, wide), jnp.float32),
            pltpu.VMEM((2 * BLK, wide), jnp.bfloat16),
            pltpu.VMEM((2, SLOTS, BLK, BLK), jnp.bfloat16),
            pltpu.VMEM((STEPS, BLK), jnp.float32),
            pltpu.VMEM((chips, STEPS, BLK), jnp.float32),
            pltpu.VMEM((layers, STEPS, BLK), jnp.float32),
            pltpu.VMEM((rows, STEPS, BLK), jnp.float32),
            pltpu.SemaphoreType.DMA((STEPS, len(MESSAGES))),
            pltpu.SemaphoreType.DMA((STEPS, len(MESSAGES))),
            pltpu.SemaphoreType.DMA,
            pltpu.SemaphoreType.DMA,
            pltpu.SemaphoreType.DMA((chips + layers + rows,)),
            pltpu.SemaphoreType.DMA((chips,)),
            pltpu.SemaphoreType.DMA((layers,)),
            pltpu.SemaphoreType.DMA((rows,)),
        ],
        compiler_params=pltpu.CompilerParams(
            collective_id=0, has_side_effects=True, vmem_limit_bytes=40 * 2**20
        ),
        name="purify",
    )(pattern, density)
    return purified, occupation


def solution(mesh):
    sizes = tuple(mesh.shape[axis] for axis in ("row", "col", "inner"))
    return jax.shard_map(
        functools.partial(on_device, sizes),
        mesh=mesh,
        in_specs=(P(("row", "col", "inner"), None), P(("row", "col", "inner"), None, None, None)),
        out_specs=(P(("row", "col", "inner"), None, None, None), P()),
        check_vma=False,
    )
```

time: 351 us -> 63.3 us (0.18)
  blocking collectives: 131 us -> 0 us
  waiting for transfers between devices: 102 us -> 0 us
  starting transfers between devices: 74.6 us -> 0 us
  Pallas kernels: 0 us -> 59.5 us
  local copies, waits for them, and re-layouts: 26.2 us -> 2.97 us
  matrix products: 10.1 us -> 0 us
  other arithmetic: 4.38 us -> 0 us
    psum x1 -> x0, blocking collectives: 131 us -> none  [on_device(): totals = lax.psum(jnp.stack(diagonal_terms), ('row', 'col', 'inner'))]
    ppermute x16 -> x0, waiting for transfers between devices: 102 us -> none  [from_behind(): lax.ppermute(value, axis, [(source, source + steps) for source in range(i...]
    ppermute x16 -> x0, starting transfers between devices: 74.6 us -> none  [from_behind(): lax.ppermute(value, axis, [(source, source + steps) for source in range(i...]
    pallas_call x0 -> x1, Pallas kernels: none -> 59.5 us  [on_device(): pl.pallas_call(functools.partial(kernel, sizes), out_shape=(jax.ShapeDtyp...]
    squeeze x3 -> x0, local copies, waits for them, and re-layouts: 14.8 us -> none  [on_device(): updated[:, REACH]]
    dot_general x40 -> x0, matrix products: 10.1 us -> none  [contract(): lax.dot_general(left, right, (((1, 3), (1, 2)), ((0,), (0,))), preferred_...]
    gather x2 -> x0, local copies, waits for them, and re-layouts: 3.92 us -> none  [on_device(): jnp.diagonal(updated[:, REACH], axis1=1, axis2=2).astype(jnp.float32)]
  transfers between devices with their start and end apart: 16 -> 0, of which waited for: 9 -> 0; matrix products, arithmetic and copies ran while one was open for 5% -> 0% of each run, Pallas kernels for 0% -> 0%
where the time goes in v1:
time: 63.3 us; the launch traced here: 63.1 us
  Pallas kernels  59.5 us (94%)
  local copies, waits for them, and re-layouts  2.97 us (5%)
  between operations  0.65 us (1%)
    pallas_call x1, Pallas kernels, on_device(): pl.pallas_call(functools.partial(kernel, sizes), out_shape=(jax.ShapeDtyp...  59.5 us
    unnamed x6, local copies, waits for them, and re-layouts  2.97 us

profile of v1, /device:TPU:1, one launch (start us, length us, event | category | flops | bytes accessed | tf_op | source)
XLA Modules:
  0.0 63.1 jit_solution(11628035801877823606)
XLA Ops:
  0.6 0.0 copy-start
  0.6 1.0 %copy-done = bf16[2,7,128,128]{3,2,1,0:T(8,128)(2,1)S(1)} copy-done((bf16[2,7,128,128]{3,2,1,0:T(8,128)(2,1)S(1)}, bf16[2,7,128,128]{3,2,1,0:T(8,128)(2,1)}, u32[]{:S(2)}) %copy-start) | copy-done | bytes 458776
  1.6 0.0 copy-start.1
  1.7 0.7 %copy-done.1 = s32[2,7]{1,0:T(2,128)S(1)} copy-done((s32[2,7]{1,0:T(2,128)S(1)}, s32[2,7]{1,0:T(2,128)}, u32[]{:S(2)}) %copy-start.1) | copy-done | bytes 80
  2.3 59.5 %purify.1 = (bf16[2,7,128,128]{3,2,1,0:T(8,128)(2,1)S(1)}, f32[2]{0:T(128)S(1)}) custom-call(s32[2,7]{1,0:T(2,128)S(1)} %copy-done.1, bf16[2,7,128,128]{3,2,1,0:T(8,128)(2,1)S(1)} %copy-done), custom_call_target="tpu_custom_call" | custom-call | tf_op jit(solution)/shard_map/purify/pallas_call | solution.py:266
  61.8 0.8 %copy.6 = bf16[2,7,128,128]{3,2,1,0:T(8,128)(2,1)} copy(bf16[2,7,128,128]{3,2,1,0:T(8,128)(2,1)S(1)} %get-tuple-element.4) | data formatting | bytes 917504
  62.6 0.5 copy.7
Async XLA Ops:
  0.6 1.0 %copy-start = (bf16[2,7,128,128]{3,2,1,0:T(8,128)(2,1)S(1)}, bf16[2,7,128,128]{3,2,1,0:T(8,128)(2,1)}, u32[]{:S(2)}) copy-start(bf16[2,7,128,128]{3,2,1,0:T(8,128)(2,1)} %density.1) | copy-start | bytes 1376260
  1.6 0.7 %copy-start.1 = (s32[2,7]{1,0:T(2,128)S(1)}, s32[2,7]{1,0:T(2,128)}, u32[]{:S(2)}) copy-start(s32[2,7]{1,0:T(2,128)} %pattern.1) | copy-start | bytes 172

commit v2 on v1

v2 whole, which is shorter than its diff:
```python
import functools

import jax
import jax.numpy as jnp
from jax import lax
from jax.experimental import pallas as pl
from jax.experimental.pallas import tpu as pltpu
from jax.sharding import PartitionSpec as P

BLK = 128
REACH = 3
SLOTS = 7
STEPS = 2
CORES = 2
MESH = pl.DeviceIdType.MESH

WINDOW = 8
COLUMNS = WINDOW + SLOTS - 1

MESSAGES = (
    (4, 0, 4, 2, 1, None),
    (3, 3, 4, 5, -1, None),
    (3, 0, 4, 1, 1, None),
    (4, 3, 4, 6, -1, None),
    (2, 0, 4, 0, 1, 0),
    (5, 3, 4, 7, -1, 1),
    (4, 6, 1, 2, 1, None),
)
FROM_OWN = ((0, 6), (1, 5), (1, 6), (2, 4), (2, 5), (5, 1), (5, 2), (6, 0), (6, 1), (7, 0))
FROM_MESSAGE = {0: ((0, 5), (1, 4)), 1: ((6, 2), (7, 1)), 2: ((0, 4),), 3: ((7, 2),), 6: ((5, 0),)}


def wrapped(index, size):
    return jnp.where(index >= size, index - size, index)


def kernel(
    sizes, pattern_in, density, purified, occupation, near0, near1, left, total, square, cross, pattern,
    bit_out, bit_in, diagonals, sums_a, sums_b, sums_c, send_sem, recv_sem, bit_sem, load_sem,
    sum_send, recv_a, recv_b, recv_c,
):
    rows, columns, inners = sizes
    count = rows * columns * inners
    layers = columns // CORES
    row, col, inner = lax.axis_index("row"), lax.axis_index("col"), lax.axis_index("inner")
    layer, core = lax.div(col, CORES), lax.rem(col, CORES)

    load = pltpu.make_async_copy(density, near0.at[pl.ds(3, 2)], load_sem.at[0])
    load.start()
    load_pattern = pltpu.make_async_copy(pattern_in, pattern, load_sem.at[1])
    load_pattern.start()

    after_col = jnp.where(inner == inners - 1, col + 1, col)
    before_col = jnp.where(inner == 0, col - 1, col)
    after = (
        wrapped(jnp.where(after_col == columns, row + 1, row), rows),
        wrapped(after_col, columns),
        wrapped(inner + 1, inners),
    )
    before = (
        wrapped(jnp.where(before_col < 0, row - 1, row) + rows, rows),
        wrapped(before_col + columns, columns),
        wrapped(inner + inners - 1, inners),
    )
    near_place = {1: after, -1: before}

    def chip(core_, inner_):
        return core_ * inners + inner_

    group_a = []
    for core_step in range(CORES):
        for step in range(inners):
            if core_step or step:
                core_ = wrapped(core + core_step, CORES)
                inner_ = wrapped(inner + step, inners)
                group_a.append(((row, layer * CORES + core_, inner_), chip(core_, inner_)))
    group_b = [
        ((row, wrapped(layer + step, layers) * CORES + core, inner), wrapped(layer + step, layers))
        for step in range(1, layers)
    ]
    order = sorted(range(1, rows), key=lambda step: -min(step, rows - step))
    group_c = [((wrapped(row + step, rows), col, inner), wrapped(row + step, rows)) for step in order]
    phase_a = (CORES * inners, chip(core, inner), group_a, sums_a, recv_a, 0)
    phase_b = (layers, layer, group_b, sums_b, recv_b, CORES * inners)
    phase_c = (rows, row, group_c, sums_c, recv_c, CORES * inners + layers)

    barrier = pltpu.get_barrier_semaphore()
    greeted = 0
    for place in (after, before):
        pl.semaphore_signal(barrier, inc=1, device_id=place, device_id_type=MESH)
        greeted += 1
    for _, _, group, _, _, _ in (phase_a, phase_c, phase_b):
        for place, _ in group:
            pl.semaphore_signal(barrier, inc=1, device_id=place, device_id_type=MESH)
            greeted += 1
    zero_block = jnp.zeros((BLK, BLK), jnp.bfloat16)
    left[0:BLK, 7 * BLK : 8 * BLK] = zero_block
    left[BLK : 2 * BLK, 0:BLK] = zero_block
    left[2 * BLK : 3 * BLK, 6 * BLK : 7 * BLK] = zero_block
    left[2 * BLK : 3 * BLK, 7 * BLK : 8 * BLK] = zero_block
    load_pattern.wait()
    bit_out[...] = jnp.full((8, BLK), jnp.where(pattern[1, 2 * REACH] == 1, 1.0, 0.0), jnp.float32)
    load.wait()
    pl.semaphore_wait(barrier, greeted)

    eye = lax.broadcasted_iota(jnp.int32, (BLK, BLK), 0) == lax.broadcasted_iota(jnp.int32, (BLK, BLK), 1)

    def block(near, r, column):
        slot = column - r
        return near[r, slot] if 0 <= slot < SLOTS else zero_block

    def tile(near, r, column, width):
        return jnp.concatenate(
            [
                jnp.concatenate([block(near, r + i, column + j) for j in range(width)], axis=1)
                for i in range(2)
            ],
            axis=0,
        )

    def mirror(near, places):
        for r, slot in places:
            near[r, slot] = near[r + slot - REACH, 2 * REACH - slot].T

    def span(column, width=2):
        return slice(column * BLK, (column + width) * BLK)

    def across(a, b):
        return lax.dot_general(a, b, (((1,), (1,)), ((), ())), preferred_element_type=jnp.float32)

    def update(near, q, store):
        cube = across(square[0 : 2 * BLK, span(2 * q, 8)], tile(near, 2 * q, 2 * q, 8))
        for r in range(2):
            for j in range(2):
                slot = 2 * q + j - r
                if 0 <= slot < SLOTS:
                    mine = span(r, 1)
                    value = (
                        3.0 * square[mine, span(2 * q + j + REACH, 1)].astype(jnp.float32)
                        - 2.0 * cube[mine, span(j, 1)]
                    )
                    store(r, slot, jnp.where(pattern[r, slot] == 1, value, 0.0).astype(jnp.bfloat16))

    def exchange(section, near):
        copies = []
        for index, (r, slot, slots, target, direction, after) in enumerate(MESSAGES):
            if section and index == 6:
                continue
            copies.append(
                pltpu.make_async_remote_copy(
                    src_ref=near.at[r, pl.ds(slot, slots)],
                    dst_ref=near.at[target, pl.ds(slot, slots)],
                    send_sem=send_sem.at[section, index],
                    recv_sem=recv_sem.at[section, index],
                    device_id=near_place[direction],
                    device_id_type=MESH,
                )
            )
            if after is None:
                copies[-1].start()
        return copies

    def fill_left(near):
        for r in range(2):
            for slot in range(SLOTS):
                left[span(r, 1), span(slot + r, 1)] = near[3 + r, slot]

    def relay(copies):
        copies[0].wait_recv()
        copies[4].start()
        copies[1].wait_recv()
        copies[5].start()

    def height(section, column):
        return 3 * BLK if section == 0 and 4 <= column < 12 else 2 * BLK

    def first_half(section, near):
        mirror(near, FROM_MESSAGE[0])
        mirror(near, FROM_MESSAGE[1])
        if section == 0:
            for slot in range(1, SLOTS):
                left[span(2, 1), span(slot - 1, 1)] = near[2, slot]
        for column in range(2, 12, 2):
            high = height(section, column)
            terms = [
                jnp.dot(left[0:high, span(r)], tile(near, r, column, 2), preferred_element_type=jnp.float32)
                for r in (2, 4)
                if r - 1 <= column <= r + 7
            ]
            total[0:high, span(column)] = functools.reduce(jnp.add, terms)

    def second_half(section, near, copies):
        copies[2].wait_recv()
        copies[3].wait_recv()
        mirror(near, FROM_MESSAGE[2])
        mirror(near, FROM_MESSAGE[3])
        copies[4].wait_recv()
        copies[5].wait_recv()
        for column in range(0, COLUMNS, 2):
            high = height(section, column)
            terms = [total[0:high, span(column)]] if 2 <= column < 12 else []
            terms += [
                jnp.dot(left[0:high, span(r)], tile(near, r, column, 2), preferred_element_type=jnp.float32)
                for r in (0, 6)
                if r - 1 <= column <= r + 7
            ]
            value = functools.reduce(jnp.add, terms)
            if section == 0 and column == 4:
                extra = across(near[2, 0], near[2, 0])
                total[span(2, 1), span(5, 1)] = value[2 * BLK : 3 * BLK, BLK : 2 * BLK] + extra
            elif high == 3 * BLK:
                total[span(2, 1), span(column)] = value[2 * BLK : 3 * BLK]
            square[:, span(column)] = value[0 : 2 * BLK].astype(jnp.bfloat16)
        if section == 0:
            cross[...] = total[span(2, 1), span(5, 7)].astype(jnp.bfloat16)

    def send_sums(phase):
        size, me, group, sums, arrived, first = phase
        sums[me] = diagonals[...]
        started = []
        for index, (place, _) in enumerate(group):
            copy = pltpu.make_async_remote_copy(
                src_ref=diagonals,
                dst_ref=sums.at[me],
                send_sem=sum_send.at[first + index],
                recv_sem=arrived.at[me],
                device_id=place,
                device_id_type=MESH,
            )
            copy.start()
            started.append(copy)
        return started

    def receive_sums(phase, started):
        size, _, group, sums, arrived, first = phase
        for index, (place, other) in enumerate(group):
            pltpu.make_async_remote_copy(
                src_ref=diagonals,
                dst_ref=sums.at[other],
                send_sem=sum_send.at[first + index],
                recv_sem=arrived.at[other],
                device_id=place,
                device_id_type=MESH,
            ).wait_recv()
        for copy in started:
            copy.wait_send()
        return functools.reduce(jnp.add, [sums[i] for i in range(size)])

    def down(value):
        return jnp.sum(value, axis=0, keepdims=True)

    copies0 = exchange(0, near0)
    bit = pltpu.make_async_remote_copy(
        src_ref=bit_out,
        dst_ref=bit_in,
        send_sem=bit_sem.at[0],
        recv_sem=bit_sem.at[1],
        device_id=after,
        device_id_type=MESH,
    )
    bit.start()
    fill_left(near0)
    mirror(near0, FROM_OWN)
    relay(copies0)
    copies0[6].wait_recv()
    mirror(near0, FROM_MESSAGE[6])
    first_half(0, near0)
    second_half(0, near0, copies0)

    def keep(r, slot, value):
        near1[3 + r, slot] = value

    for q in range(4):
        update(near0, q, keep)
    copies1 = exchange(1, near1)
    bit.wait_recv()
    value = 3.0 * cross[:, span(3, 1)].astype(jnp.float32) - 2.0 * across(
        cross[...], jnp.concatenate([near0[5, slot] for slot in range(SLOTS)], axis=1)
    )
    near1[2, 6] = jnp.where(bit_in[0:1, :] == 1.0, value, 0.0).astype(jnp.bfloat16)
    fill_left(near1)

    diagonals[0:1, :] = down(
        sum(jnp.where(eye, near1[3 + r, REACH].astype(jnp.float32), 0.0) for r in range(2))
    )
    squares = sum(near1[3 + r, slot].astype(jnp.float32) ** 2 for r in range(2) for slot in range(SLOTS))
    own = left[0 : 2 * BLK, span(3)]
    outer = jnp.concatenate([left[0 : 2 * BLK, span(0, 3)], left[0 : 2 * BLK, span(5, 3)]], axis=1)
    gram = across(own, own) + 3.0 * across(outer, outer)
    cubes = own.astype(jnp.float32) * gram
    cubes = cubes[:, 0:BLK] + cubes[:, BLK : 2 * BLK]
    far = jnp.dot(left[0 : 2 * BLK, span(2, 1)], near1[2, 6], preferred_element_type=jnp.float32)
    cubes += 6.0 * far * left[0 : 2 * BLK, span(5, 1)].astype(jnp.float32)
    diagonals[1:2, :] = 3.0 * down(squares) - 2.0 * down(cubes)

    started = send_sums(phase_a)
    mirror(near1, FROM_OWN)
    mirror(near1, FROM_MESSAGE[6])
    diagonals[...] = receive_sums(phase_a, started)
    started = send_sums(phase_c)
    relay(copies1)
    first_half(1, near1)
    diagonals[...] = receive_sums(phase_c, started)
    started = send_sums(phase_b)
    second_half(1, near1, copies1)

    def finish(r, slot, value):
        purified[r, slot] = value

    for q in range(4):
        update(near1, q, finish)
    for copy in copies0 + copies1:
        copy.wait_send()
    bit.wait_send()
    occupation[...] = receive_sums(phase_b, started)


def on_device(sizes, pattern, density):
    rows, columns, inners = sizes
    chips, layers = CORES * inners, columns // CORES
    flat = pltpu.VMEM((WINDOW, SLOTS, BLK, BLK), jnp.bfloat16)
    wide = COLUMNS * BLK
    purified, sums = pl.pallas_call(
        functools.partial(kernel, sizes),
        out_shape=(
            pltpu.VMEM(density.shape, jnp.bfloat16),
            pltpu.VMEM((STEPS, BLK), jnp.float32),
        ),
        in_specs=[pl.BlockSpec(memory_space=pltpu.HBM), pl.BlockSpec(memory_space=pltpu.HBM)],
        out_specs=(pl.BlockSpec(memory_space=pltpu.VMEM), pl.BlockSpec(memory_space=pltpu.VMEM)),
        scratch_shapes=[
            flat,
            flat,
            pltpu.VMEM((3 * BLK, WINDOW * BLK), jnp.bfloat16),
            pltpu.VMEM((3 * BLK, wide), jnp.float32),
            pltpu.VMEM((2 * BLK, wide), jnp.bfloat16),
            pltpu.VMEM((BLK, SLOTS * BLK), jnp.bfloat16),
            pltpu.SMEM((2, SLOTS), jnp.int32),
            pltpu.VMEM((8, BLK), jnp.float32),
            pltpu.VMEM((8, BLK), jnp.float32),
            pltpu.VMEM((STEPS, BLK), jnp.float32),
            pltpu.VMEM((chips, STEPS, BLK), jnp.float32),
            pltpu.VMEM((layers, STEPS, BLK), jnp.float32),
            pltpu.VMEM((rows, STEPS, BLK), jnp.float32),
            pltpu.SemaphoreType.DMA((STEPS, len(MESSAGES))),
            pltpu.SemaphoreType.DMA((STEPS, len(MESSAGES))),
            pltpu.SemaphoreType.DMA((2,)),
            pltpu.SemaphoreType.DMA((2,)),
            pltpu.SemaphoreType.DMA((chips + layers + rows,)),
            pltpu.SemaphoreType.DMA((chips,)),
            pltpu.SemaphoreType.DMA((layers,)),
            pltpu.SemaphoreType.DMA((rows,)),
        ],
        compiler_params=pltpu.CompilerParams(
            collective_id=0, has_side_effects=True, vmem_limit_bytes=56 * 2**20
        ),
        name="purify",
    )(pattern, density)
    order = 2.0 * BLK * rows * columns * inners
    return purified, jnp.sum(sums, axis=1) / order


def solution(mesh):
    sizes = tuple(mesh.shape[axis] for axis in ("row", "col", "inner"))
    return jax.shard_map(
        functools.partial(on_device, sizes),
        mesh=mesh,
        in_specs=(P(("row", "col", "inner"), None), P(("row", "col", "inner"), None, None, None)),
        out_specs=(P(("row", "col", "inner"), None, None, None), P()),
        check_vma=False,
    )
```

time: 63.3 us -> 52.5 us (0.83)
  Pallas kernels: 59.5 us -> 50.3 us
  local copies, waits for them, and re-layouts: 2.97 us -> 0.77 us
    pallas_call x1, Pallas kernels: 59.5 us -> 50.3 us  [on_device(): pl.pallas_call(functools.partial(kernel, sizes), out_shape=(pltpu.VMEM(de...]
    unnamed x6 -> x1, local copies, waits for them, and re-layouts: 2.97 us -> 0.77 us
where the time goes in v2:
time: 52.5 us; the launch traced here: 52.3 us
  Pallas kernels  50.3 us (96%)
  local copies, waits for them, and re-layouts  0.77 us (1%)
  between operations  0.64 us (1%)
  other arithmetic  0.63 us (1%)
    pallas_call x1, Pallas kernels, on_device(): pl.pallas_call(functools.partial(kernel, sizes), out_shape=(pltpu.VMEM(de...  50.3 us

profile of v2, /device:TPU:1, one launch (start us, length us, event | category | flops | bytes accessed | tf_op | source)
XLA Modules:
  0.0 52.3 jit_solution(2730059951926751419)
XLA Ops:
  0.6 50.3 %purify.1 = (bf16[2,7,128,128]{3,2,1,0:T(8,128)(2,1)S(1)}, f32[2,128]{1,0:T(2,128)S(1)}) custom-call(s32[2,7]{1,0:T(2,128)} %pattern_in.1, bf16[2,7,128,128]{3,2,1,0:T(8,128)(2,1)} %density.1), custom_call_target="tpu_custom_call" | custom-call | tf_op jit(solution)/shard_map/purify/pallas_call | solution.py:323
  50.9 0.8 %copy.5 = bf16[2,7,128,128]{3,2,1,0:T(8,128)(2,1)} copy(bf16[2,7,128,128]{3,2,1,0:T(8,128)(2,1)S(1)} %get-tuple-element.6) | data formatting | bytes 917504
  51.7 0.1 reduce_sum.9
  51.8 0.5 broadcast_multiply_fusion

commit v3 on v2

--- a/solution.py
+++ b/solution.py
@@ -36,7 +36,7 @@
 
 def kernel(
     sizes, pattern_in, density, purified, occupation, near0, near1, left, total, square, cross, pattern,
-    bit_out, bit_in, diagonals, sums_a, sums_b, sums_c, send_sem, recv_sem, bit_sem, load_sem,
+    bit_out, bit_in, sums_a, sums_b, sums_c, send_sem, recv_sem, bit_sem, load_sem,
     sum_send, recv_a, recv_b, recv_c,
 ):
     rows, columns, inners = sizes
@@ -100,7 +100,6 @@
     left[2 * BLK : 3 * BLK, 7 * BLK : 8 * BLK] = zero_block
     load_pattern.wait()
     bit_out[...] = jnp.full((8, BLK), jnp.where(pattern[1, 2 * REACH] == 1, 1.0, 0.0), jnp.float32)
-    load.wait()
     pl.semaphore_wait(barrier, greeted)
 
     eye = lax.broadcasted_iota(jnp.int32, (BLK, BLK), 0) == lax.broadcasted_iota(jnp.int32, (BLK, BLK), 1)
@@ -148,7 +147,9 @@
                 continue
             copies.append(
                 pltpu.make_async_remote_copy(
-                    src_ref=near.at[r, pl.ds(slot, slots)],
+                    src_ref=density.at[r - 3, pl.ds(slot, slots)]
+                    if section == 0 and after is None
+                    else near.at[r, pl.ds(slot, slots)],
                     dst_ref=near.at[target, pl.ds(slot, slots)],
                     send_sem=send_sem.at[section, index],
                     recv_sem=recv_sem.at[section, index],
@@ -216,11 +217,10 @@
 
     def send_sums(phase):
         size, me, group, sums, arrived, first = phase
-        sums[me] = diagonals[...]
         started = []
         for index, (place, _) in enumerate(group):
             copy = pltpu.make_async_remote_copy(
-                src_ref=diagonals,
+                src_ref=sums.at[me],
                 dst_ref=sums.at[me],
                 send_sem=sum_send.at[first + index],
                 recv_sem=arrived.at[me],
@@ -231,19 +231,17 @@
             started.append(copy)
         return started
 
-    def receive_sums(phase, started):
-        size, _, group, sums, arrived, first = phase
+    def receive_sums(phase):
+        size, me, group, sums, arrived, first = phase
         for index, (place, other) in enumerate(group):
             pltpu.make_async_remote_copy(
-                src_ref=diagonals,
+                src_ref=sums.at[me],
                 dst_ref=sums.at[other],
                 send_sem=sum_send.at[first + index],
                 recv_sem=arrived.at[other],
                 device_id=place,
                 device_id_type=MESH,
             ).wait_recv()
-        for copy in started:
-            copy.wait_send()
         return functools.reduce(jnp.add, [sums[i] for i in range(size)])
 
     def down(value):
@@ -259,6 +257,7 @@
         device_id_type=MESH,
     )
     bit.start()
+    load.wait()
     fill_left(near0)
     mirror(near0, FROM_OWN)
     relay(copies0)
@@ -272,7 +271,6 @@
 
     for q in range(4):
         update(near0, q, keep)
-    copies1 = exchange(1, near1)
     bit.wait_recv()
     value = 3.0 * cross[:, span(3, 1)].astype(jnp.float32) - 2.0 * across(
         cross[...], jnp.concatenate([near0[5, slot] for slot in range(SLOTS)], axis=1)
@@ -280,7 +278,7 @@
     near1[2, 6] = jnp.where(bit_in[0:1, :] == 1.0, value, 0.0).astype(jnp.bfloat16)
     fill_left(near1)
 
-    diagonals[0:1, :] = down(
+    sums_a[phase_a[1], 0:1] = down(
         sum(jnp.where(eye, near1[3 + r, REACH].astype(jnp.float32), 0.0) for r in range(2))
     )
     squares = sum(near1[3 + r, slot].astype(jnp.float32) ** 2 for r in range(2) for slot in range(SLOTS))
@@ -291,17 +289,18 @@
     cubes = cubes[:, 0:BLK] + cubes[:, BLK : 2 * BLK]
     far = jnp.dot(left[0 : 2 * BLK, span(2, 1)], near1[2, 6], preferred_element_type=jnp.float32)
     cubes += 6.0 * far * left[0 : 2 * BLK, span(5, 1)].astype(jnp.float32)
-    diagonals[1:2, :] = 3.0 * down(squares) - 2.0 * down(cubes)
-
-    started = send_sums(phase_a)
+    sums_a[phase_a[1], 1:2] = 3.0 * down(squares) - 2.0 * down(cubes)
+
+    sent = send_sums(phase_a)
+    copies1 = exchange(1, near1)
     mirror(near1, FROM_OWN)
     mirror(near1, FROM_MESSAGE[6])
-    diagonals[...] = receive_sums(phase_a, started)
-    started = send_sums(phase_c)
+    sums_c[phase_c[1]] = receive_sums(phase_a)
+    sent += send_sums(phase_c)
     relay(copies1)
     first_half(1, near1)
-    diagonals[...] = receive_sums(phase_c, started)
-    started = send_sums(phase_b)
+    sums_b[phase_b[1]] = receive_sums(phase_c)
+    sent += send_sums(phase_b)
     second_half(1, near1, copies1)
 
     def finish(r, slot, value):
@@ -309,10 +308,11 @@
 
     for q in range(4):
         update(near1, q, finish)
-    for copy in copies0 + copies1:
+    for copy in copies0 + copies1 + [bit] + sent[: len(group_a) + len(group_c)]:
         copy.wait_send()
-    bit.wait_send()
-    occupation[...] = receive_sums(phase_b, started)
+    occupation[...] = receive_sums(phase_b)
+    for copy in sent[len(group_a) + len(group_c) :]:
+        copy.wait_send()
 
 
 def on_device(sizes, pattern, density):
@@ -338,7 +338,6 @@
             pltpu.SMEM((2, SLOTS), jnp.int32),
             pltpu.VMEM((8, BLK), jnp.float32),
             pltpu.VMEM((8, BLK), jnp.float32),
-            pltpu.VMEM((STEPS, BLK), jnp.float32),
             pltpu.VMEM((chips, STEPS, BLK), jnp.float32),
             pltpu.VMEM((layers, STEPS, BLK), jnp.float32),
             pltpu.VMEM((rows, STEPS, BLK), jnp.float32),

time: 52.5 us -> 50.1 us (0.954)
  Pallas kernels: 50.3 us -> 47.9 us
    pallas_call x1, Pallas kernels: 50.3 us -> 47.9 us  [on_device(): pl.pallas_call(functools.partial(kernel, sizes), out_shape=(pltpu.VMEM(de...]
where the time goes in v3:
time: 50.1 us; the launch traced here: 50 us
  Pallas kernels  47.9 us (96%)
  local copies, waits for them, and re-layouts  0.77 us (2%)
  between operations  0.64 us (1%)
  other arithmetic  0.63 us (1%)
    pallas_call x1, Pallas kernels, on_device(): pl.pallas_call(functools.partial(kernel, sizes), out_shape=(pltpu.VMEM(de...  47.9 us

profile of v3, /device:TPU:1, one launch (start us, length us, event | category | flops | bytes accessed | tf_op | source)
XLA Modules:
  0.0 50.0 jit_solution(6760681313066136279)
XLA Ops:
  0.6 47.9 %purify.1 = (bf16[2,7,128,128]{3,2,1,0:T(8,128)(2,1)S(1)}, f32[2,128]{1,0:T(2,128)S(1)}) custom-call(s32[2,7]{1,0:T(2,128)} %pattern_in.1, bf16[2,7,128,128]{3,2,1,0:T(8,128)(2,1)} %density.1), custom_call_target="tpu_custom_call" | custom-call | tf_op jit(solution)/shard_map/purify/pallas_call | solution.py:323
  48.6 0.8 %copy.5 = bf16[2,7,128,128]{3,2,1,0:T(8,128)(2,1)} copy(bf16[2,7,128,128]{3,2,1,0:T(8,128)(2,1)S(1)} %get-tuple-element.6) | data formatting | bytes 917504
  49.3 0.1 reduce_sum.9
  49.5 0.5 %broadcast_multiply_fusion = f32[2]{0:T(128)} fusion(f32[2]{0:T(128)S(1)} %reduce_sum.9), kind=kLoop, calls=%fused_computation | loop fusion | flops 2 | bytes 16 | tf_op jit(solution)/shard_map/div | solution.py:359

commit v4 on v3

--- a/solution.py
+++ b/solution.py
@@ -37,7 +37,7 @@
 def kernel(
     sizes, pattern_in, density, purified, occupation, near0, near1, left, total, square, cross, pattern,
     bit_out, bit_in, sums_a, sums_b, sums_c, send_sem, recv_sem, bit_sem, load_sem,
-    sum_send, recv_a, recv_b, recv_c,
+    sum_send, recv_a, recv_b, recv_c, in_above, in_below,
 ):
     rows, columns, inners = sizes
     count = rows * columns * inners
@@ -89,10 +89,21 @@
     for place in (after, before):
         pl.semaphore_signal(barrier, inc=1, device_id=place, device_id_type=MESH)
         greeted += 1
-    for _, _, group, _, _, _ in (phase_a, phase_c, phase_b):
-        for place, _ in group:
-            pl.semaphore_signal(barrier, inc=1, device_id=place, device_id_type=MESH)
-            greeted += 1
+    lines = []
+    for axis, (size, at) in enumerate(
+        (
+            (rows, lambda step: (wrapped(row + step, rows), col, inner)),
+            (layers, lambda step: (row, wrapped(layer + step, layers) * CORES + core, inner)),
+        )
+    ):
+        if size > 1:
+            lines.append((axis, size, at(1), at(size - 1)))
+    greetings = [place for place, _ in group_a]
+    for _, size, above, below in lines:
+        greetings += [above] if size == 2 else [above, below]
+    for place in greetings:
+        pl.semaphore_signal(barrier, inc=1, device_id=place, device_id_type=MESH)
+        greeted += 1
     zero_block = jnp.zeros((BLK, BLK), jnp.bfloat16)
     left[0:BLK, 7 * BLK : 8 * BLK] = zero_block
     left[BLK : 2 * BLK, 0:BLK] = zero_block
@@ -101,6 +112,22 @@
     load_pattern.wait()
     bit_out[...] = jnp.full((8, BLK), jnp.where(pattern[1, 2 * REACH] == 1, 1.0, 0.0), jnp.float32)
     pl.semaphore_wait(barrier, greeted)
+
+    def spread(turn):
+        for axis, size, above, below in lines:
+            if turn < size // 2 - 1:
+                pl.semaphore_signal(in_above.at[axis, turn], inc=1, device_id=below, device_id_type=MESH)
+            if turn < (size - 1) // 2 - 1:
+                pl.semaphore_signal(in_below.at[axis, turn], inc=1, device_id=above, device_id_type=MESH)
+
+    def learn(turn):
+        for axis, size, above, below in lines:
+            if turn < size // 2 - 1:
+                pl.semaphore_wait(in_above.at[axis, turn], 1)
+            if turn < (size - 1) // 2 - 1:
+                pl.semaphore_wait(in_below.at[axis, turn], 1)
+
+    turns = max([size // 2 - 1 for _, size, _, _ in lines] + [0])
 
     eye = lax.broadcasted_iota(jnp.int32, (BLK, BLK), 0) == lax.broadcasted_iota(jnp.int32, (BLK, BLK), 1)
 
@@ -195,6 +222,9 @@
         copies[3].wait_recv()
         mirror(near, FROM_MESSAGE[2])
         mirror(near, FROM_MESSAGE[3])
+        if section == 0:
+            learn(3)
+            spread(4)
         copies[4].wait_recv()
         copies[5].wait_recv()
         for column in range(0, COLUMNS, 2):
@@ -257,13 +287,20 @@
         device_id_type=MESH,
     )
     bit.start()
+    spread(0)
     load.wait()
     fill_left(near0)
     mirror(near0, FROM_OWN)
+    learn(0)
+    spread(1)
     relay(copies0)
+    learn(1)
+    spread(2)
     copies0[6].wait_recv()
     mirror(near0, FROM_MESSAGE[6])
     first_half(0, near0)
+    learn(2)
+    spread(3)
     second_half(0, near0, copies0)
 
     def keep(r, slot, value):
@@ -300,6 +337,9 @@
     relay(copies1)
     first_half(1, near1)
     sums_b[phase_b[1]] = receive_sums(phase_c)
+    for turn in range(4, turns):
+        learn(turn)
+        spread(turn + 1)
     sent += send_sums(phase_b)
     second_half(1, near1, copies1)
 
@@ -349,6 +389,8 @@
             pltpu.SemaphoreType.DMA((chips,)),
             pltpu.SemaphoreType.DMA((layers,)),
             pltpu.SemaphoreType.DMA((rows,)),
+            pltpu.SemaphoreType.REGULAR((2, max(rows, layers))),
+            pltpu.SemaphoreType.REGULAR((2, max(rows, layers))),
         ],
         compiler_params=pltpu.CompilerParams(
             collective_id=0, has_side_effects=True, vmem_limit_bytes=56 * 2**20

time: 50.1 us -> 46.9 us (0.936)
  Pallas kernels: 47.9 us -> 44.7 us
    pallas_call x1, Pallas kernels: 47.9 us -> 44.7 us  [on_device(): pl.pallas_call(functools.partial(kernel, sizes), out_shape=(pltpu.VMEM(de...]
where the time goes in v4:
time: 46.9 us; the launch traced here: 46.8 us
  Pallas kernels  44.7 us (95%)
  local copies, waits for them, and re-layouts  0.77 us (2%)
  between operations  0.64 us (1%)
  other arithmetic  0.63 us (1%)
    pallas_call x1, Pallas kernels, on_device(): pl.pallas_call(functools.partial(kernel, sizes), out_shape=(pltpu.VMEM(de...  44.7 us

profile of v4, /device:TPU:1, one launch (start us, length us, event | category | flops | bytes accessed | tf_op | source)
XLA Modules:
  0.0 46.8 jit_solution(6049017013754289594)
XLA Ops:
  0.6 44.7 %purify.1 = (bf16[2,7,128,128]{3,2,1,0:T(8,128)(2,1)S(1)}, f32[2,128]{1,0:T(2,128)S(1)}) custom-call(s32[2,7]{1,0:T(2,128)} %pattern_in.1, bf16[2,7,128,128]{3,2,1,0:T(8,128)(2,1)} %density.1), custom_call_target="tpu_custom_call" | custom-call | tf_op jit(solution)/shard_map/purify/pallas_call | solution.py:363
  45.4 0.8 %copy.5 = bf16[2,7,128,128]{3,2,1,0:T(8,128)(2,1)} copy(bf16[2,7,128,128]{3,2,1,0:T(8,128)(2,1)S(1)} %get-tuple-element.6) | data formatting | bytes 917504
  46.1 0.1 reduce_sum.9
  46.2 0.5 %broadcast_multiply_fusion = f32[2]{0:T(128)} fusion(f32[2]{0:T(128)S(1)} %reduce_sum.9), kind=kLoop, calls=%fused_computation | loop fusion | flops 2 | bytes 16 | tf_op jit(solution)/shard_map/div | solution.py:401

commit v5 on v4

--- a/solution.py
+++ b/solution.py
@@ -18,16 +18,23 @@
 COLUMNS = WINDOW + SLOTS - 1
 
 MESSAGES = (
-    (4, 0, 4, 2, 1, None),
-    (3, 3, 4, 5, -1, None),
-    (3, 0, 4, 1, 1, None),
-    (4, 3, 4, 6, -1, None),
-    (2, 0, 4, 0, 1, 0),
-    (5, 3, 4, 7, -1, 1),
-    (4, 6, 1, 2, 1, None),
+    (4, 0, 2, 2, 1),
+    (3, 5, 2, 5, -1),
+    (4, 2, 2, 2, 1),
+    (3, 3, 2, 5, -1),
+    (3, 0, 4, 1, 1),
+    (4, 3, 4, 6, -1),
+    (4, 6, 1, 2, 1),
+    (2, 0, 2, 0, 1),
+    (5, 5, 2, 7, -1),
+    (2, 2, 2, 0, 1),
+    (5, 3, 2, 7, -1),
 )
+PASSED = 4
 FROM_OWN = ((0, 6), (1, 5), (1, 6), (2, 4), (2, 5), (5, 1), (5, 2), (6, 0), (6, 1), (7, 0))
-FROM_MESSAGE = {0: ((0, 5), (1, 4)), 1: ((6, 2), (7, 1)), 2: ((0, 4),), 3: ((7, 2),), 6: ((5, 0),)}
+FROM_PASSED = ((0, 5), (1, 4), (6, 2), (7, 1))
+FROM_FAR = ((0, 4), (7, 2))
+FROM_CROSS = ((5, 0),)
 
 
 def wrapped(index, size):
@@ -169,14 +176,11 @@
 
     def exchange(section, near):
         copies = []
-        for index, (r, slot, slots, target, direction, after) in enumerate(MESSAGES):
-            if section and index == 6:
-                continue
+        for index, (r, slot, slots, target, direction) in enumerate(MESSAGES):
+            source = density.at[r - 3] if section == 0 and index < 7 else near.at[r]
             copies.append(
                 pltpu.make_async_remote_copy(
-                    src_ref=density.at[r - 3, pl.ds(slot, slots)]
-                    if section == 0 and after is None
-                    else near.at[r, pl.ds(slot, slots)],
+                    src_ref=source.at[pl.ds(slot, slots)],
                     dst_ref=near.at[target, pl.ds(slot, slots)],
                     send_sem=send_sem.at[section, index],
                     recv_sem=recv_sem.at[section, index],
@@ -184,9 +188,17 @@
                     device_id_type=MESH,
                 )
             )
-            if after is None:
+            if index < PASSED:
                 copies[-1].start()
         return copies
+
+    def follow(section, copies):
+        copies[0].wait_send()
+        if section == 0:
+            copies[6].start()
+        copies[4].start()
+        copies[1].wait_send()
+        copies[5].start()
 
     def fill_left(near):
         for r in range(2):
@@ -194,17 +206,15 @@
                 left[span(r, 1), span(slot + r, 1)] = near[3 + r, slot]
 
     def relay(copies):
-        copies[0].wait_recv()
-        copies[4].start()
-        copies[1].wait_recv()
-        copies[5].start()
+        for index in range(PASSED):
+            copies[index].wait_recv()
+            copies[index + 7].start()
 
     def height(section, column):
         return 3 * BLK if section == 0 and 4 <= column < 12 else 2 * BLK
 
     def first_half(section, near):
-        mirror(near, FROM_MESSAGE[0])
-        mirror(near, FROM_MESSAGE[1])
+        mirror(near, FROM_PASSED)
         if section == 0:
             for slot in range(1, SLOTS):
                 left[span(2, 1), span(slot - 1, 1)] = near[2, slot]
@@ -218,15 +228,14 @@
             total[0:high, span(column)] = functools.reduce(jnp.add, terms)
 
     def second_half(section, near, copies):
-        copies[2].wait_recv()
-        copies[3].wait_recv()
-        mirror(near, FROM_MESSAGE[2])
-        mirror(near, FROM_MESSAGE[3])
+        copies[4].wait_recv()
+        copies[5].wait_recv()
+        mirror(near, FROM_FAR)
         if section == 0:
             learn(3)
             spread(4)
-        copies[4].wait_recv()
-        copies[5].wait_recv()
+        for index in range(7, 11):
+            copies[index].wait_recv()
         for column in range(0, COLUMNS, 2):
             high = height(section, column)
             terms = [total[0:high, span(column)]] if 2 <= column < 12 else []
@@ -288,6 +297,7 @@
     )
     bit.start()
     spread(0)
+    follow(0, copies0)
     load.wait()
     fill_left(near0)
     mirror(near0, FROM_OWN)
@@ -297,7 +307,7 @@
     learn(1)
     spread(2)
     copies0[6].wait_recv()
-    mirror(near0, FROM_MESSAGE[6])
+    mirror(near0, FROM_CROSS)
     first_half(0, near0)
     learn(2)
     spread(3)
@@ -330,8 +340,9 @@
 
     sent = send_sums(phase_a)
     copies1 = exchange(1, near1)
+    follow(1, copies1)
     mirror(near1, FROM_OWN)
-    mirror(near1, FROM_MESSAGE[6])
+    mirror(near1, FROM_CROSS)
     sums_c[phase_c[1]] = receive_sums(phase_a)
     sent += send_sums(phase_c)
     relay(copies1)
@@ -348,7 +359,7 @@
 
     for q in range(4):
         update(near1, q, finish)
-    for copy in copies0 + copies1 + [bit] + sent[: len(group_a) + len(group_c)]:
+    for copy in copies0[2:] + copies1[2:6] + copies1[7:] + [bit] + sent[: len(group_a) + len(group_c)]:
         copy.wait_send()
     occupation[...] = receive_sums(phase_b)
     for copy in sent[len(group_a) + len(group_c) :]:

time: 46.9 us -> 46.4 us (0.989)
  Pallas kernels: 44.7 us -> 44.2 us
    pallas_call x1, Pallas kernels: 44.7 us -> 44.2 us  [on_device(): pl.pallas_call(functools.partial(kernel, sizes), out_shape=(pltpu.VMEM(de...]
where the time goes in v5:
time: 46.4 us; the launch traced here: 46.2 us
  Pallas kernels  44.2 us (95%)
  local copies, waits for them, and re-layouts  0.77 us (2%)
  between operations  0.64 us (1%)
  other arithmetic  0.63 us (1%)
    pallas_call x1, Pallas kernels, on_device(): pl.pallas_call(functools.partial(kernel, sizes), out_shape=(pltpu.VMEM(de...  44.2 us

profile of v5, /device:TPU:1, one launch (start us, length us, event | category | flops | bytes accessed | tf_op | source)
XLA Modules:
  0.0 46.2 jit_solution(12018750038320383975)
XLA Ops:
  0.6 44.2 %purify.1 = (bf16[2,7,128,128]{3,2,1,0:T(8,128)(2,1)S(1)}, f32[2,128]{1,0:T(2,128)S(1)}) custom-call(s32[2,7]{1,0:T(2,128)} %pattern_in.1, bf16[2,7,128,128]{3,2,1,0:T(8,128)(2,1)} %density.1), custom_call_target="tpu_custom_call" | custom-call | tf_op jit(solution)/shard_map/purify/pallas_call | solution.py:374
  44.8 0.8 %copy.5 = bf16[2,7,128,128]{3,2,1,0:T(8,128)(2,1)} copy(bf16[2,7,128,128]{3,2,1,0:T(8,128)(2,1)S(1)} %get-tuple-element.6) | data formatting | bytes 917504
  45.6 0.1 reduce_sum.9
  45.7 0.5 %broadcast_multiply_fusion = f32[2]{0:T(128)} fusion(f32[2]{0:T(128)S(1)} %reduce_sum.9), kind=kLoop, calls=%fused_computation | loop fusion | flops 2 | bytes 16 | tf_op jit(solution)/shard_map/div | solution.py:412

commit v6 on v5

--- a/solution.py
+++ b/solution.py
@@ -346,12 +346,12 @@
     sums_c[phase_c[1]] = receive_sums(phase_a)
     sent += send_sums(phase_c)
     relay(copies1)
-    first_half(1, near1)
     sums_b[phase_b[1]] = receive_sums(phase_c)
     for turn in range(4, turns):
         learn(turn)
         spread(turn + 1)
     sent += send_sums(phase_b)
+    first_half(1, near1)
     second_half(1, near1, copies1)
 
     def finish(r, slot, value):

time: 46.4 us -> 46.4 us (level)
  no operation moved by 1% of the time
where the time goes in v6:
time: 46.4 us; the launch traced here: 46.2 us
  Pallas kernels  44.2 us (95%)
  local copies, waits for them, and re-layouts  0.77 us (2%)
  between operations  0.64 us (1%)
  other arithmetic  0.63 us (1%)
    pallas_call x1, Pallas kernels, on_device(): pl.pallas_call(functools.partial(kernel, sizes), out_shape=(pltpu.VMEM(de...  44.2 us

profile of v6, /device:TPU:1, one launch (start us, length us, event | category | flops | bytes accessed | tf_op | source)
XLA Modules:
  0.0 46.2 jit_solution(11616911642397897332)
XLA Ops:
  0.6 44.2 %purify.1 = (bf16[2,7,128,128]{3,2,1,0:T(8,128)(2,1)S(1)}, f32[2,128]{1,0:T(2,128)S(1)}) custom-call(s32[2,7]{1,0:T(2,128)} %pattern_in.1, bf16[2,7,128,128]{3,2,1,0:T(8,128)(2,1)} %density.1), custom_call_target="tpu_custom_call" | custom-call | tf_op jit(solution)/shard_map/purify/pallas_call | solution.py:374
  44.8 0.8 %copy.5 = bf16[2,7,128,128]{3,2,1,0:T(8,128)(2,1)} copy(bf16[2,7,128,128]{3,2,1,0:T(8,128)(2,1)S(1)} %get-tuple-element.6) | data formatting | bytes 917504
  45.6 0.1 reduce_sum.9
  45.7 0.5 %broadcast_multiply_fusion = f32[2]{0:T(128)} fusion(f32[2]{0:T(128)S(1)} %reduce_sum.9), kind=kLoop, calls=%fused_computation | loop fusion | flops 2 | bytes 16 | tf_op jit(solution)/shard_map/div | solution.py:412

commit v7 on v5

--- a/solution.py
+++ b/solution.py
@@ -18,17 +18,17 @@
 COLUMNS = WINDOW + SLOTS - 1
 
 MESSAGES = (
-    (4, 0, 2, 2, 1),
-    (3, 5, 2, 5, -1),
-    (4, 2, 2, 2, 1),
-    (3, 3, 2, 5, -1),
+    (4, 0, 1, 2, 1),
+    (3, 6, 1, 5, -1),
+    (4, 1, 3, 2, 1),
+    (3, 3, 3, 5, -1),
     (3, 0, 4, 1, 1),
     (4, 3, 4, 6, -1),
     (4, 6, 1, 2, 1),
-    (2, 0, 2, 0, 1),
-    (5, 5, 2, 7, -1),
-    (2, 2, 2, 0, 1),
-    (5, 3, 2, 7, -1),
+    (2, 0, 1, 0, 1),
+    (5, 6, 1, 7, -1),
+    (2, 1, 3, 0, 1),
+    (5, 3, 3, 7, -1),
 )
 PASSED = 4
 FROM_OWN = ((0, 6), (1, 5), (1, 6), (2, 4), (2, 5), (5, 1), (5, 2), (6, 0), (6, 1), (7, 0))

time: 46.4 us -> 46.4 us (level)
  no operation moved by 1% of the time
where the time goes in v7:
time: 46.4 us; the launch traced here: 46.3 us
  Pallas kernels  44.2 us (95%)
  local copies, waits for them, and re-layouts  0.77 us (2%)
  between operations  0.64 us (1%)
  other arithmetic  0.63 us (1%)
    pallas_call x1, Pallas kernels, on_device(): pl.pallas_call(functools.partial(kernel, sizes), out_shape=(pltpu.VMEM(de...  44.2 us

profile of v7, /device:TPU:1, one launch (start us, length us, event | category | flops | bytes accessed | tf_op | source)
XLA Modules:
  0.0 46.3 jit_solution(3558005449855837809)
XLA Ops:
  0.6 44.2 %purify.1 = (bf16[2,7,128,128]{3,2,1,0:T(8,128)(2,1)S(1)}, f32[2,128]{1,0:T(2,128)S(1)}) custom-call(s32[2,7]{1,0:T(2,128)} %pattern_in.1, bf16[2,7,128,128]{3,2,1,0:T(8,128)(2,1)} %density.1), custom_call_target="tpu_custom_call" | custom-call | tf_op jit(solution)/shard_map/purify/pallas_call | solution.py:374
  44.9 0.8 %copy.5 = bf16[2,7,128,128]{3,2,1,0:T(8,128)(2,1)} copy(bf16[2,7,128,128]{3,2,1,0:T(8,128)(2,1)S(1)} %get-tuple-element.6) | data formatting | bytes 917504
  45.6 0.1 reduce_sum.9
  45.8 0.5 %broadcast_multiply_fusion = f32[2]{0:T(128)} fusion(f32[2]{0:T(128)S(1)} %reduce_sum.9), kind=kLoop, calls=%fused_computation | loop fusion | flops 2 | bytes 16 | tf_op jit(solution)/shard_map/div | solution.py:412
